TPU v7x, 32 devices: a whole 2x2x4 slice. The times are simulated.
32 devices in a mesh: row: 8 (over z, y), col: 4 (over x, core).
Axes of the slice: x: 2, y: 2, z: 4, core: 2. Of those that a mesh axis runs over, the one named last changes fastest.
Arguments:
- sim_window: bfloat16 [1536, 1536], P('row', 'col'), as said below
- sim_rest: bfloat16 [1536, 118464], P('row', 'col'), may hold values from -6 to 6
- joined_partner_pairs: int32 [192, 2], replicated, may hold values from 0 to 1535, as said below
- cluster_member_count: int32 [1536], replicated, may hold values from 1 to 64
Outputs:
- window_out: bfloat16 [1536, 1536], P('row', 'col')
- rest_out: bfloat16 [1536, 118464], P('row', 'col')
Inputs may be any that keep to these rules, and one draw needn't show every extreme that they name: `joined_partner_pairs`: each row is (survivor, partner); no window item appears twice in the whole list. Each aligned block of 192 items holds exactly 24 partners. For any two aligned blocks (possibly the same), at most 3 pairs have their partner in the first and their survivor in the second, and some two blocks have exactly 3. Nearly symmetric: sim_window[i, j] is close to sim_window[j, i].
All inputs are finite; a program needn't handle non-finite values.
Results may differ from a plain program's by a relative error of at most 0.001.
Values may be sent and summed in bfloat16 or wider, within the bound.
A program may use at most 128 MiB of HBM per device.

v0:
```python
import jax
import jax.numpy as jnp
from jax import lax
from jax.sharding import PartitionSpec as P


def pairing_tables(joined_partner_pairs, cluster_member_count):
    lasting_node = joined_partner_pairs[:, 0]
    vanishing_node = joined_partner_pairs[:, 1]
    remaining_size = cluster_member_count[lasting_node].astype(jnp.float32)
    absorbed_size = cluster_member_count[vanishing_node].astype(jnp.float32)
    joined_cluster_size = remaining_size + absorbed_size
    return (
        lasting_node,
        vanishing_node,
        remaining_size / joined_cluster_size,
        absorbed_size / joined_cluster_size,
    )


def item_weight_values(node_labels, lasting_node, vanishing_node, retained_pair, selected_pair):
    lasting_mask = node_labels[:, None] == lasting_node[None, :]
    belongs_mask = node_labels[:, None] == vanishing_node[None, :]
    lasting_real_mask = lasting_mask.astype(jnp.float32)
    matched_mask = jnp.sum((lasting_mask | belongs_mask).astype(jnp.float32), axis=1)
    retained_entries = (
        1.0 - matched_mask + jnp.sum(lasting_real_mask * retained_pair[None, :], axis=1)
    )
    selected_entries = jnp.sum(lasting_real_mask * selected_pair[None, :], axis=1)
    donor_position = jnp.sum(jnp.where(lasting_mask, vanishing_node[None, :], 0), axis=1)
    return (retained_entries, selected_entries, donor_position)


def shards(sim_window, sim_rest, joined_partner_pairs, cluster_member_count):
    row_number_total = sim_window.shape[0]
    col_count = sim_window.shape[1]
    blocks = lax.axis_size("row")
    local_block = lax.axis_index("row")
    my_col = lax.axis_index("col")
    lasting_node, vanishing_node, retained_pair, selected_pair = pairing_tables(
        joined_partner_pairs, cluster_member_count
    )
    row_sequence = jnp.arange(row_number_total, dtype=jnp.int32)
    retained_entries, selected_entries, ignored = item_weight_values(
        local_block * row_number_total + row_sequence,
        lasting_node,
        vanishing_node,
        retained_pair,
        selected_pair,
    )
    src_block = vanishing_node // row_number_total
    destination_block = lasting_node // row_number_total
    pair_count = joined_partner_pairs.shape[0]
    pair_order = jnp.arange(pair_count, dtype=jnp.int32)
    earlier = pair_order[None, :] < pair_order[:, None]
    slot_width = row_number_total // 64
    same_route = (src_block[None, :] == src_block[:, None]) & (
        destination_block[None, :] == destination_block[:, None]
    )
    slot_rank = jnp.sum((earlier & same_route).astype(jnp.int32), axis=1)
    send_slot = destination_block * slot_width + slot_rank
    send_width = blocks * slot_width
    recv_slot = src_block * slot_width + slot_rank
    recv_width = blocks * slot_width
    mine_src = src_block == local_block
    slot_hot = (
        (jnp.arange(send_width, dtype=jnp.int32)[:, None] == send_slot[None, :]) & mine_src[None, :]
    ).astype(jnp.bfloat16)
    row_hot = (
        (vanishing_node - local_block * row_number_total)[:, None] == row_sequence[None, :]
    ).astype(jnp.bfloat16)
    selector = jnp.dot(slot_hot, row_hot, preferred_element_type=jnp.float32).astype(jnp.bfloat16)
    send_window = jnp.dot(selector, sim_window, preferred_element_type=jnp.float32).astype(
        jnp.bfloat16
    )
    send_rest = jnp.dot(selector, sim_rest, preferred_element_type=jnp.float32).astype(jnp.bfloat16)
    local_destination = destination_block == local_block
    target_hot = (
        ((lasting_node - local_block * row_number_total)[None, :] == row_sequence[:, None])
        & local_destination[None, :]
    ).astype(jnp.bfloat16)
    recv_hot = (recv_slot[:, None] == jnp.arange(recv_width, dtype=jnp.int32)[None, :]).astype(
        jnp.bfloat16
    )
    placement = jnp.dot(target_hot, recv_hot, preferred_element_type=jnp.float32).astype(
        jnp.bfloat16
    )
    got_window, got_rest = (
        lax.all_to_all(send_window, "row", split_axis=0, concat_axis=0, tiled=True),
        lax.all_to_all(send_rest, "row", split_axis=0, concat_axis=0, tiled=True),
    )
    placed_window = jnp.dot(placement, got_window, preferred_element_type=jnp.float32)
    placed_rest = jnp.dot(placement, got_rest, preferred_element_type=jnp.float32)
    mixed_window = (
        retained_entries[:, None] * sim_window.astype(jnp.float32)
        + selected_entries[:, None] * placed_window
    ).astype(jnp.bfloat16)
    rest_out = (
        retained_entries[:, None] * sim_rest.astype(jnp.float32)
        + selected_entries[:, None] * placed_rest
    ).astype(jnp.bfloat16)
    col_iota = jnp.arange(col_count, dtype=jnp.int32)
    column_identifiers = my_col * col_count + col_iota
    column_retained, column_selected, column_provider = item_weight_values(
        column_identifiers, lasting_node, vanishing_node, retained_pair, selected_pair
    )
    piece = lax.all_gather(mixed_window, "col", axis=1, tiled=True)
    piece_width = piece.shape[1]
    picker = (jnp.arange(piece_width, dtype=jnp.int32)[:, None] == column_provider[None, :]).astype(
        jnp.bfloat16
    )
    gathered = jnp.dot(piece, picker, preferred_element_type=jnp.float32)
    window_out = (
        column_retained[None, :] * mixed_window.astype(jnp.float32)
        + column_selected[None, :] * gathered
    ).astype(jnp.bfloat16)
    return (window_out, rest_out)


def solution(mesh):
    in_specs = (P("row", "col"), P("row", "col"), P(), P())
    out_specs = (P("row", "col"), P("row", "col"))
    return jax.shard_map(shards, mesh=mesh, in_specs=in_specs, out_specs=out_specs, check_vma=False)
```

profile of v0, /device:TPU:0, one launch (start us, length us, event | category | flops | bytes accessed | tf_op | source)
XLA Modules:
  0.0 81.8 jit_solution(13757915902915737448)
XLA Ops:
  0.6 0.0 copy-start
  0.7 0.8 compare_select_fusion.6
  1.5 0.2 convert_reduce_fusion.1
  1.7 0.2 convolution_convert_fusion.2
  1.9 1.1 %convolution_convert_fusion.1 = bf16[24,384]{1,0:T(8,128)(2,1)S(1)} fusion(bf16[24,192]{1,0:T(8,128)(2,1)S(1)} %convolution_convert_fusion.2, bf16[192,384]{1,0:T(8,128)(2,1)} %param.4), kind=kOutput, calls=%fused_computation.15 | convolution fusion | flops 3548160 | bytes 175104 | tf_op jit(solution)/shard_map/dot_general | solution.py:73
  3.0 0.6 all_to_all.16
  3.6 7.3 %all-to-all-start = ((bf16[8,3,384]{2,1,0:T(4,128)(2,1)}), bf16[8,3,384]{2,1,0:T(4,128)(2,1)S(1)}, u32[]{:S(2)}, u32[]{:S(2)}) async-start(bf16[8,3,384]{2,1,0:T(4,128)(2,1)} %all_to_all.16), calls=%async_computation | async-start | bytes 49152 | tf_op jit(solution)/shard_map/all_to_all | solution.py:89
  10.9 5.9 %convolution_convert_fusion = bf16[24,29616]{1,0:T(8,128)(2,1)S(1)} fusion(bf16[24,192]{1,0:T(8,128)(2,1)S(1)} %convolution_convert_fusion.2, bf16[192,29616]{1,0:T(8,128)(2,1)} %param.5), kind=kOutput, calls=%fused_computation.5 | convolution fusion | flops 273651840 | bytes 12803328 | tf_op jit(solution)/shard_map/dot_general | solution.py:76
  16.8 2.0 %all_to_all.19 = bf16[8,3,29616]{2,1,0:T(4,128)(2,1)} reshape(bf16[24,29616]{1,0:T(8,128)(2,1)S(1)} %convolution_convert_fusion) | data formatting | bytes 2843136 | tf_op jit(solution)/shard_map/all_to_all | solution.py:90
  18.8 0.0 copy-done
  18.9 1.4 %gather_fusion = s32[192]{0:T(256)S(1)} fusion(s32[1536]{0:T(1024)S(1)} %copy-done, s32[1024]{0:T(1024)S(1)} %pad_clamp_fusion.1), kind=kCustom, calls=%fused_computation | custom fusion | bytes 2304 | tf_op jit(solution)/shard_map/gather | solution.py:10
  20.3 1.4 %gather_fusion.1 = s32[192]{0:T(256)S(1)} fusion(s32[1536]{0:T(1024)S(1)} %copy-done, s32[1024]{0:T(1024)S(1)} %pad_clamp_fusion), kind=kCustom, calls=%fused_computation.1 | custom fusion | bytes 2304 | tf_op jit(solution)/shard_map/gather | solution.py:11
  21.7 0.0 all-to-all-done
  21.8 6.0 %all-to-all-start.1 = ((bf16[8,3,29616]{2,1,0:T(4,128)(2,1)}), bf16[8,3,29616]{2,1,0:T(4,128)(2,1)S(1)}, u32[]{:S(2)}, u32[]{:S(2)}) async-start(bf16[8,3,29616]{2,1,0:T(4,128)(2,1)} %all_to_all.19), calls=%async_computation.1 | async-start | bytes 3801088 | tf_op jit(solution)/shard_map/all_to_all | solution.py:90
  27.8 0.1 fusion.11
  27.9 0.3 convert_reduce_fusion.2
  28.2 0.2 convert_reduce_fusion
  28.4 0.2 convolution_convert_fusion.3
  28.7 0.2 fusion.8
  29.0 7.5 %all_gather.3 = bf16[192,1536]{1,0:T(8,128)(2,1)S(1)} all-gather(bf16[192,384]{1,0:T(8,128)(2,1)S(1)} %fusion.8), channel_id=1, replica_groups=mesh['row'=8,'col'=4] {'col'}, dimensions={1}, use_global_device_ids=true | all-gather | bytes 737280 | tf_op jit(solution)/shard_map/all_gather | solution.py:107
  36.5 1.3 %fusion.7 = bf16[192,384]{1,0:T(8,128)(2,1)} fusion(bf16[192,1536]{1,0:T(8,128)(2,1)S(1)} %all_gather.3, s32[384]{0:T(512)S(1)} %fusion.11, bf16[192,384]{1,0:T(8,128)(2,1)S(1)} %fusion.8, f32[384]{0:T(512)S(1)} %get-tuple-element.4, f32[384]{0:T(512)S(1)} %subtract_add_fusion), kind=kOutput, calls=%fused_computation.13 | convolution fusion | flops 227450880 | bytes 889344 | tf_op jit(solution)/shard_map/dot_general | solution.py:112
  37.7 33.5 %all-to-all-done.1 = bf16[8,3,29616]{2,1,0:T(4,128)(2,1)S(1)} async-done(((bf16[8,3,29616]{2,1,0:T(4,128)(2,1)}), bf16[8,3,29616]{2,1,0:T(4,128)(2,1)S(1)}, u32[]{:S(2)}, u32[]{:S(2)}) %all-to-all-start.1) | async-done | bytes 1421600 | tf_op jit(solution)/shard_map/all_to_all | solution.py:90
  71.2 1.2 %all_to_all.21 = bf16[24,29616]{1,0:T(8,128)(2,1)S(1)} reshape(bf16[8,3,29616]{2,1,0:T(4,128)(2,1)S(1)} %all-to-all-done.1) | data formatting | bytes 2843136 | tf_op jit(solution)/shard_map/all_to_all | solution.py:90
  72.4 9.4 %fusion.1 = bf16[192,29616]{1,0:T(8,128)(2,1)} fusion(bf16[192,24]{0,1:T(8,128)(2,1)S(1)} %convolution_convert_fusion.3, bf16[24,29616]{1,0:T(8,128)(2,1)S(1)} %all_to_all.21, bf16[192,29616]{1,0:T(8,128)(2,1)} %param.5, f32[192]{0:T(256)S(1)} %get-tuple-element.6, f32[192]{0:T(256)S(1)} %subtract_add_fusion.1), kind=kOutput, calls=%fused_computation.4 | convolution fusion | flops 301372416 | bytes 24177408 | tf_op jit(solution)/shard_map/dot_general | solution.py:93
  (14 shorter events, 0.1 us)
Async XLA Ops:
  0.6 18.2 %copy-start = (s32[1536]{0:T(1024)S(1)}, s32[1536]{0:T(1024)}, u32[]{:S(2)}) copy-start(s32[1536]{0:T(1024)} %param.7) | copy-start | bytes 18436
  3.6 18.2 %all-to-all-start = ((bf16[8,3,384]{2,1,0:T(4,128)(2,1)}), bf16[8,3,384]{2,1,0:T(4,128)(2,1)S(1)}, u32[]{:S(2)}, u32[]{:S(2)}) async-start(bf16[8,3,384]{2,1,0:T(4,128)(2,1)} %all_to_all.16), calls=%async_computation | async-start | bytes 49152 | tf_op jit(solution)/shard_map/all_to_all | solution.py:89
  10.9 17.8 %copy-start.1 = (bf16[192,384]{1,0:T(8,128)(2,1)S(1)}, bf16[192,384]{1,0:T(8,128)(2,1)}, u32[]{:S(2)}) copy-start(bf16[192,384]{1,0:T(8,128)(2,1)} %param.4) | copy-start | bytes 442372
  21.8 49.5 %all-to-all-start.1 = ((bf16[8,3,29616]{2,1,0:T(4,128)(2,1)}), bf16[8,3,29616]{2,1,0:T(4,128)(2,1)S(1)}, u32[]{:S(2)}, u32[]{:S(2)}) async-start(bf16[8,3,29616]{2,1,0:T(4,128)(2,1)} %all_to_all.19), calls=%async_computation.1 | async-start | bytes 3801088 | tf_op jit(solution)/shard_map/all_to_all | solution.py:90
where the time goes:
time: 82.1 us; the launch traced here: 81.8 us
  waiting for transfers between devices  33.5 us (41%)
  matrix products  18.2 us (22%)
  starting transfers between devices  13.3 us (16%)
  blocking collectives  7.53 us (9%)
  local copies, waits for them, and re-layouts  6.78 us (8%)
  other arithmetic  1.66 us (2%)
    all_to_all x1, waiting for transfers between devices, shards(): lax.all_to_all(send_rest, 'row', split_axis=0, concat_axis=0, tiled=True)  33.5 us
    dot_general x1, matrix products, shards(): jnp.dot(placement, got_rest, preferred_element_type=jnp.float32)  9.36 us
    all_gather x1, blocking collectives, shards(): piece = lax.all_gather(mixed_window, 'col', axis=1, tiled=True)  7.53 us
    all_to_all x1, starting transfers between devices, shards(): lax.all_to_all(send_window, 'row', split_axis=0, concat_axis=0, tiled=True)  7.28 us
    all_to_all x1, starting transfers between devices, shards(): lax.all_to_all(send_rest, 'row', split_axis=0, concat_axis=0, tiled=True)  6 us
    dot_general x1, matrix products, shards(): jnp.dot(selector, sim_rest, preferred_element_type=jnp.float32)  5.87 us
    all_to_all x2, local copies, waits for them, and re-layouts, shards(): lax.all_to_all(send_rest, 'row', split_axis=0, concat_axis=0, tiled=True)  3.22 us
  transfers between devices with their start and end apart: 2, of which 1 were waited for; matrix products, arithmetic and copies ran while one was open for 14% of the time, Pallas kernels for 0%

commit v1 on v0

v1 whole, which is shorter than its diff:
```python
import functools

import jax
import jax.numpy as jnp
from jax import lax
from jax.experimental import pallas as pl
from jax.experimental.pallas import tpu as pltpu
from jax.sharding import PartitionSpec as P

LANES = 128
GROUP = 8
STRIP = 2048
STRIPS = 2
MESH = pl.DeviceIdType.MESH


def transfer_rows(width, slots):
    tiles = -(-width // LANES)
    return -(-(tiles * slots) // 16) * 16


def iota(shape, axis):
    return lax.broadcasted_iota(jnp.int32, shape, axis)


def pack_strip(chosen, staging, width, slots):
    for start in range(0, width, LANES):
        tile = start // LANES
        stop = min(start + LANES, width)
        staging[:, slots * tile : slots * (tile + 1), 0 : stop - start] = chosen[
            :, 0:slots, start:stop
        ]


def unpack_strip(staging, spread, width, slots):
    for start in range(0, width, LANES):
        tile = start // LANES
        stop = min(start + LANES, width)
        spread[:, 0:slots, start:stop] = staging[
            :, slots * tile : slots * (tile + 1), 0 : stop - start
        ]


def merge_kernel(
    blocks,
    col_blocks,
    slots,
    window_ref,
    rest_ref,
    pairs_ref,
    count_ref,
    window_out,
    rest_out,
    send_main,
    got_main,
    send_tail,
    got_tail,
    send_win,
    got_win,
    mixed,
    staging,
    spread,
    place_ref,
    keep_ref,
    take_ref,
    load_sem,
    send_sem,
    recv_sem,
    col_send_sem,
    col_recv_sem,
):
    rows, window_cols = window_ref.shape
    cols = rest_ref.shape[1]
    pair_count = pairs_ref.shape[0]
    chunk = STRIP * STRIPS
    chunks = cols // chunk
    tail = cols - chunks * chunk
    strip_rows = slots * (STRIP // LANES)
    me = lax.axis_index("row")
    my_col = lax.axis_index("col")
    order = sorted(range(1, blocks), key=lambda m: (abs(m - blocks // 2), m))

    loads = [
        pltpu.make_async_copy(
            rest_ref.at[:, pl.ds(c * chunk, chunk)],
            rest_out.at[:, pl.ds(c * chunk, chunk)],
            load_sem.at[c],
        )
        for c in range(chunks)
    ]
    if tail:
        loads.append(
            pltpu.make_async_copy(
                rest_ref.at[:, pl.ds(chunks * chunk, tail)],
                rest_out.at[:, pl.ds(chunks * chunk, tail)],
                load_sem.at[chunks],
            )
        )
    for load in loads:
        load.start()

    barrier = pltpu.get_barrier_semaphore()
    for m in range(1, blocks):
        pl.semaphore_signal(
            barrier, inc=1, device_id=(lax.rem(me + m, blocks), my_col), device_id_type=MESH
        )
    for m in range(1, col_blocks):
        pl.semaphore_signal(
            barrier, inc=1, device_id=(me, lax.rem(my_col + m, col_blocks)), device_id_type=MESH
        )

    survivor_s = pairs_ref[:, 0:1]
    partner_s = pairs_ref[:, 1:2]
    square = (pair_count, pair_count)
    diagonal = iota(square, 0) == iota(square, 1)

    def along_lanes(column):
        return jnp.sum(jnp.where(diagonal, column, jnp.zeros_like(column)), axis=0, keepdims=True)

    def block_of(items):
        block = jnp.zeros_like(items)
        for b in range(1, blocks):
            block = block + (items >= b * rows).astype(jnp.int32)
        return block

    survivor_l = along_lanes(survivor_s)
    partner_l = along_lanes(partner_s)
    src_s, src_l = block_of(partner_s), block_of(partner_l)
    dst_s, dst_l = block_of(survivor_s), block_of(survivor_l)
    same = (src_s * blocks + dst_s) == (src_l * blocks + dst_l)
    rank_l = jnp.sum(
        jnp.where(same & (iota(square, 0) < iota(square, 1)), 1, 0), axis=0, keepdims=True
    )
    rank_s = jnp.sum(
        jnp.where(same & (iota(square, 1) < iota(square, 0)), 1, 0), axis=1, keepdims=True
    )
    slot_shape = (blocks * GROUP, pair_count)
    slot_hot = (iota(slot_shape, 0) == dst_l * GROUP + rank_l) & (src_l == me)
    row_hot = (partner_s - me * rows) == iota((pair_count, rows), 1)
    selector = jnp.dot(
        jnp.where(slot_hot, 1.0, 0.0).astype(jnp.bfloat16),
        jnp.where(row_hot, 1.0, 0.0).astype(jnp.bfloat16),
        preferred_element_type=jnp.float32,
    ).astype(jnp.bfloat16)

    staging[...] = jnp.zeros_like(staging)

    def choose(values, width):
        chosen = jnp.dot(selector, values, preferred_element_type=jnp.float32)
        pack_strip(chosen.reshape(blocks, GROUP, width), staging, width, slots)

    def row_copy(src, dst, index, peer, slot):
        return pltpu.make_async_remote_copy(
            src_ref=src,
            dst_ref=dst,
            send_sem=send_sem.at[index, peer],
            recv_sem=recv_sem.at[index, slot],
            device_id=(peer, my_col),
            device_id_type=MESH,
        )

    win_rows = send_win.shape[1]
    choose(window_ref[...], window_cols)
    send_win[...] = staging[:, 0:win_rows, :].astype(jnp.bfloat16)
    got_win[me] = send_win[me]
    pl.semaphore_wait(barrier, blocks - 1 + col_blocks - 1)
    for m in order:
        peer = lax.rem(me + m, blocks)
        row_copy(send_win.at[peer], got_win.at[me], chunks + 1, peer, me).start()

    def send_chunk(c, carry):
        pltpu.make_async_copy(
            rest_ref.at[:, pl.ds(0, chunk)], rest_out.at[:, pl.ds(0, chunk)], load_sem.at[c]
        ).wait()
        for j in range(STRIPS):
            first = pl.multiple_of(c * chunk + j * STRIP, LANES)
            choose(rest_out[:, pl.ds(first, STRIP)], STRIP)
            send_main[c, :, j * strip_rows : (j + 1) * strip_rows, :] = staging[
                :, 0:strip_rows, :
            ].astype(jnp.bfloat16)
        for m in order:
            peer = lax.rem(me + m, blocks)
            row_copy(send_main.at[c, peer], got_main.at[c, me], c, peer, me).start()
        got_main[c, me] = send_main[c, me]
        return carry

    lax.fori_loop(0, chunks, send_chunk, 0)

    tail_strips = [(s, min(STRIP, tail - s)) for s in range(0, tail, STRIP)]
    if tail:
        loads[chunks].wait()
        for start, width in tail_strips:
            choose(rest_out[:, chunks * chunk + start : chunks * chunk + start + width], width)
            at = slots * (start // LANES)
            size = transfer_rows(width, slots)
            send_tail[:, at : at + size, :] = staging[:, 0:size, :].astype(jnp.bfloat16)
        for m in order:
            peer = lax.rem(me + m, blocks)
            row_copy(send_tail.at[peer], got_tail.at[me], chunks, peer, me).start()
        got_tail[me] = send_tail[me]

    recv_hot = iota((pair_count, blocks * GROUP), 1) == src_s * GROUP + rank_s
    target_hot = (survivor_l - me * rows) == iota((rows, pair_count), 0)
    place_ref[...] = jnp.dot(
        jnp.where(target_hot, 1.0, 0.0).astype(jnp.bfloat16),
        jnp.where(recv_hot, 1.0, 0.0).astype(jnp.bfloat16),
        preferred_element_type=jnp.float32,
    ).astype(jnp.bfloat16)

    lanes_shape = (pair_count, LANES)

    def look_up(step, sums):
        kept, gone = sums
        first = pl.multiple_of(step * LANES, LANES)
        counts = count_ref[:, pl.ds(first, LANES)]
        item = iota(lanes_shape, 1) + step * LANES
        return (
            kept + jnp.where(item == survivor_s, counts, 0),
            gone + jnp.where(item == partner_s, counts, 0),
        )

    zeros = jnp.zeros(lanes_shape, jnp.int32)
    kept, gone = lax.fori_loop(0, count_ref.shape[1] // LANES, look_up, (zeros, zeros))
    kept = jnp.sum(kept, axis=1, keepdims=True).astype(jnp.float32)
    gone = jnp.sum(gone, axis=1, keepdims=True).astype(jnp.float32)
    retained_s = kept / (kept + gone)
    selected_s = gone / (kept + gone)
    retained_l, selected_l = along_lanes(retained_s), along_lanes(selected_s)

    item_rows = me * rows + iota((rows, pair_count), 0)
    survives = item_rows == survivor_l
    vanishes = item_rows == partner_l
    keep_ref[...] = jnp.broadcast_to(
        1.0
        - jnp.sum(jnp.where(survives | vanishes, 1.0, 0.0), axis=1, keepdims=True)
        + jnp.sum(jnp.where(survives, retained_l, 0.0), axis=1, keepdims=True),
        keep_ref.shape,
    )
    take_ref[...] = jnp.broadcast_to(
        jnp.sum(jnp.where(survives, selected_l, 0.0), axis=1, keepdims=True), take_ref.shape
    )
    item_cols = my_col * window_cols + iota((pair_count, window_cols), 1)
    survives = item_cols == survivor_s
    vanishes = item_cols == partner_s
    col_keep = (
        1.0
        - jnp.sum(jnp.where(survives | vanishes, 1.0, 0.0), axis=0, keepdims=True)
        + jnp.sum(jnp.where(survives, retained_s, 0.0), axis=0, keepdims=True)
    )
    col_take = jnp.sum(jnp.where(survives, selected_s, 0.0), axis=0, keepdims=True)
    col_source = jnp.sum(jnp.where(survives, partner_s, 0), axis=0, keepdims=True)

    spread[...] = jnp.zeros_like(spread)

    def mix(own, width):
        unpack_strip(staging, spread, width, slots)
        moved = spread[:, :, 0:width].reshape(blocks * GROUP, width).astype(jnp.bfloat16)
        placed = jnp.dot(place_ref[...], moved, preferred_element_type=jnp.float32)
        return (
            keep_ref[:, 0:1] * own.astype(jnp.float32) + take_ref[:, 0:1] * placed
        ).astype(jnp.bfloat16)

    for m in order:
        peer = lax.rem(me + m, blocks)
        row_copy(send_win.at[peer], got_win.at[peer], chunks + 1, peer, peer).wait_recv()
    staging[:, 0:win_rows, :] = got_win[...].astype(jnp.float32)
    mixed[my_col] = mix(window_ref[...], window_cols)

    def col_copy(source, peer):
        return pltpu.make_async_remote_copy(
            src_ref=mixed.at[my_col],
            dst_ref=mixed.at[source],
            send_sem=col_send_sem.at[peer],
            recv_sem=col_recv_sem.at[source],
            device_id=(me, peer),
            device_id_type=MESH,
        )

    for m in range(1, col_blocks):
        col_copy(my_col, lax.rem(my_col + m, col_blocks)).start()

    def mix_chunk(c, carry):
        for m in order:
            peer = lax.rem(me + m, blocks)
            row_copy(send_main.at[c, peer], got_main.at[c, peer], c, peer, peer).wait_recv()
        for j in range(STRIPS):
            first = pl.multiple_of(c * chunk + j * STRIP, LANES)
            staging[:, 0:strip_rows, :] = got_main[
                c, :, j * strip_rows : (j + 1) * strip_rows, :
            ].astype(jnp.float32)
            rest_out[:, pl.ds(first, STRIP)] = mix(rest_out[:, pl.ds(first, STRIP)], STRIP)
        return carry

    def finish_window():
        for m in range(1, col_blocks):
            peer = lax.rem(my_col + m, col_blocks)
            col_copy(peer, peer).wait_recv()

        def gather(b, total):
            picker = (iota((window_cols, window_cols), 0) + b * window_cols) == col_source
            return total + jnp.dot(
                mixed[b],
                jnp.where(picker, 1.0, 0.0).astype(jnp.bfloat16),
                preferred_element_type=jnp.float32,
            )

        gathered = lax.fori_loop(
            0, col_blocks, gather, jnp.zeros((rows, window_cols), jnp.float32)
        )
        window_out[...] = (
            col_keep * mixed[my_col].astype(jnp.float32) + col_take * gathered
        ).astype(jnp.bfloat16)

    half = chunks // 2
    lax.fori_loop(0, half, mix_chunk, 0)
    finish_window()
    lax.fori_loop(half, chunks, mix_chunk, 0)

    if tail:
        for m in order:
            peer = lax.rem(me + m, blocks)
            row_copy(send_tail.at[peer], got_tail.at[peer], chunks, peer, peer).wait_recv()
        for start, width in tail_strips:
            at = slots * (start // LANES)
            size = transfer_rows(width, slots)
            staging[:, 0:size, :] = got_tail[:, at : at + size, :].astype(jnp.float32)
            place = slice(chunks * chunk + start, chunks * chunk + start + width)
            rest_out[:, place] = mix(rest_out[:, place], width)

    def drain(c, carry):
        for m in order:
            peer = lax.rem(me + m, blocks)
            row_copy(send_main.at[c, peer], got_main.at[c, me], c, peer, me).wait_send()
        return carry

    lax.fori_loop(0, chunks, drain, 0)
    for m in order:
        peer = lax.rem(me + m, blocks)
        row_copy(send_win.at[peer], got_win.at[me], chunks + 1, peer, me).wait_send()
        if tail:
            row_copy(send_tail.at[peer], got_tail.at[me], chunks, peer, me).wait_send()
    for m in range(1, col_blocks):
        col_copy(my_col, lax.rem(my_col + m, col_blocks)).wait_send()


def shards(sim_window, sim_rest, joined_partner_pairs, cluster_member_count):
    blocks = lax.axis_size("row")
    col_blocks = lax.axis_size("col")
    rows, window_cols = sim_window.shape
    cols = sim_rest.shape[1]
    slots = rows // 64
    chunk = STRIP * STRIPS
    chunks = cols // chunk
    tail = cols - chunks * chunk
    main_rows = slots * (chunk // LANES)
    tail_rows = max(16, transfer_rows(tail, slots))
    win_rows = transfer_rows(window_cols, slots)
    stage_rows = max(slots * (STRIP // LANES), win_rows)
    bf16, f32 = jnp.bfloat16, jnp.float32
    vmem = pl.BlockSpec(memory_space=pltpu.VMEM)
    return pl.pallas_call(
        functools.partial(merge_kernel, blocks, col_blocks, slots),
        out_shape=(
            jax.ShapeDtypeStruct(sim_window.shape, bf16),
            jax.ShapeDtypeStruct(sim_rest.shape, bf16),
        ),
        in_specs=[vmem, pl.BlockSpec(memory_space=pl.ANY), vmem, vmem],
        out_specs=(vmem, vmem),
        scratch_shapes=[
            pltpu.VMEM((chunks, blocks, main_rows, LANES), bf16),
            pltpu.VMEM((chunks, blocks, main_rows, LANES), bf16),
            pltpu.VMEM((blocks, tail_rows, LANES), bf16),
            pltpu.VMEM((blocks, tail_rows, LANES), bf16),
            pltpu.VMEM((blocks, win_rows, LANES), bf16),
            pltpu.VMEM((blocks, win_rows, LANES), bf16),
            pltpu.VMEM((col_blocks, rows, window_cols), bf16),
            pltpu.VMEM((blocks, stage_rows, LANES), f32),
            pltpu.VMEM((blocks, GROUP, STRIP), f32),
            pltpu.VMEM((rows, blocks * GROUP), bf16),
            pltpu.VMEM((rows, LANES), f32),
            pltpu.VMEM((rows, LANES), f32),
            pltpu.SemaphoreType.DMA((chunks + 1,)),
            pltpu.SemaphoreType.DMA((chunks + 2, blocks)),
            pltpu.SemaphoreType.DMA((chunks + 2, blocks)),
            pltpu.SemaphoreType.DMA((col_blocks,)),
            pltpu.SemaphoreType.DMA((col_blocks,)),
        ],
        compiler_params=pltpu.CompilerParams(
            collective_id=0, has_side_effects=True, vmem_limit_bytes=44 * 1024 * 1024
        ),
        name="merge",
    )(sim_window, sim_rest, joined_partner_pairs, cluster_member_count.reshape(1, -1))


def solution(mesh):
    in_specs = (P("row", "col"), P("row", "col"), P(), P())
    out_specs = (P("row", "col"), P("row", "col"))
    return jax.shard_map(shards, mesh=mesh, in_specs=in_specs, out_specs=out_specs, check_vma=False)
```

time: 82.1 us -> 59.2 us (0.72)
  Pallas kernels: 0 us -> 45.5 us
  waiting for transfers between devices: 33.5 us -> 0 us
  matrix products: 18.2 us -> 0 us
  starting transfers between devices: 13.3 us -> 0 us
  blocking collectives: 7.53 us -> 0 us
  local copies, waits for them, and re-layouts: 6.78 us -> 12.8 us
  other arithmetic: 1.66 us -> 0 us
    pallas_call x0 -> x1, Pallas kernels: none -> 45.5 us  [shards(): pl.pallas_call(functools.partial(merge_kernel, blocks, col_blocks, slots)...]
    all_to_all x2 -> x0, waiting for transfers between devices: 33.5 us -> none  [the longest x1 33.5 us: shards(): lax.all_to_all(send_rest, 'row', split_axis=0, concat_axis=0, tiled=True)]
    dot_general x7 -> x0, matrix products: 18.2 us -> none  [the longest x1 9.36 us: shards(): jnp.dot(placement, got_rest, preferred_element_type=jnp.float32)]
    all_to_all x2 -> x0, starting transfers between devices: 13.3 us -> none  [the longest x1 7.28 us: shards(): lax.all_to_all(send_window, 'row', split_axis=0, concat_axis=0, tiled=True)]
    unnamed x4 -> x5, local copies, waits for them, and re-layouts: 0.01 us -> 12.1 us
    all_gather x1 -> x0, blocking collectives: 7.53 us -> none  [shards(): piece = lax.all_gather(mixed_window, 'col', axis=1, tiled=True)]
    all_to_all x4 -> x0, local copies, waits for them, and re-layouts: 3.89 us -> none  [the longest x2 3.22 us: shards(): lax.all_to_all(send_rest, 'row', split_axis=0, concat_axis=0, tiled=True)]
    gather x2 -> x0, local copies, waits for them, and re-layouts: 2.88 us -> none  [the longest x1 1.44 us: pairing_tables(): absorbed_size = cluster_member_count[vanishing_node].astype(jnp.float32)]
  transfers between devices with their start and end apart: 2 -> 0, of which waited for: 1 -> 0; matrix products, arithmetic and copies ran while one was open for 14% -> 0% of each run, Pallas kernels for 0% -> 0%
where the time goes in v1:
time: 59.2 us; the launch traced here: 59 us
  Pallas kernels  45.5 us (77%)
  local copies, waits for them, and re-layouts  12.8 us (22%)
  between operations  0.65 us (1%)
    pallas_call x1, Pallas kernels, shards(): pl.pallas_call(functools.partial(merge_kernel, blocks, col_blocks, slots)...  45.5 us
    unnamed x5, local copies, waits for them, and re-layouts  12.1 us

profile of v1, /device:TPU:0, one launch (start us, length us, event | category | flops | bytes accessed | tf_op | source)
XLA Modules:
  0.0 59.0 jit_solution(5269124569958701179)
XLA Ops:
  0.6 0.7 %reshape.7.count_ref = s32[1,1536]{1,0:T(1,128)S(1)} reshape(s32[1536]{0:T(1024)} %param.7) | data formatting | bytes 12288 | tf_op jit(solution)/shard_map/reshape | solution.py:392
  1.3 0.8 %copy.6.pairs_ref = s32[192,2]{1,0:T(8,128)S(1)} copy(s32[192,2]{0,1:T(2,128)} %param.6) | data formatting | bytes 3072 | tf_op args[2]
  2.1 0.0 copy-start
  2.1 0.9 %copy-done = bf16[192,384]{1,0:T(8,128)(2,1)S(1)} copy-done((bf16[192,384]{1,0:T(8,128)(2,1)S(1)}, bf16[192,384]{1,0:T(8,128)(2,1)}, u32[]{:S(2)}) %copy-start) | copy-done | bytes 147480
  3.0 45.5 %merge.1 = (bf16[192,384]{1,0:T(8,128)(2,1)S(1)}, bf16[192,29616]{1,0:T(8,128)(2,1)}) custom-call(bf16[192,384]{1,0:T(8,128)(2,1)S(1)} %copy-done, bf16[192,29616]{1,0:T(8,128)(2,1)} %rest_ref.1, s32[192,2]{1,0:T(8,128)S(1)} %copy.6.pairs_ref, s32[1,1536]{1,0:T(1,128)S(1)} %reshape.7.count_ref), custom_call_target="tpu_custom_call" | custom-call | tf_op jit(solution)/shard_map/merge/pallas_call | solution.py:361
  48.6 0.7 %copy.9 = bf16[192,384]{1,0:T(8,128)(2,1)} copy(bf16[192,384]{1,0:T(8,128)(2,1)S(1)} %get-tuple-element.4) | data formatting | bytes 294912
  49.2 9.8 %copy.10 = bf16[192,29616]{1,0:T(8,128)(2,1)} copy(bf16[192,29616]{1,0:T(8,128)(2,1)} %get-tuple-element.5) | data formatting | bytes 22745088
Async XLA Ops:
  2.1 0.9 %copy-start = (bf16[192,384]{1,0:T(8,128)(2,1)S(1)}, bf16[192,384]{1,0:T(8,128)(2,1)}, u32[]{:S(2)}) copy-start(bf16[192,384]{1,0:T(8,128)(2,1)} %window_ref.1) | copy-start | bytes 442372

commit v2 on v1

--- a/solution.py
+++ b/solution.py
@@ -10,7 +10,7 @@
 LANES = 128
 GROUP = 8
 STRIP = 2048
-STRIPS = 2
+STRIPS = 4
 MESH = pl.DeviceIdType.MESH
 
 
@@ -45,10 +45,10 @@
     blocks,
     col_blocks,
     slots,
-    window_ref,
+    window_hbm,
     rest_ref,
-    pairs_ref,
-    count_ref,
+    pairs_hbm,
+    count_hbm,
     window_out,
     rest_out,
     send_main,
@@ -57,21 +57,26 @@
     got_tail,
     send_win,
     got_win,
+    window_ref,
+    pairs_ref,
+    count_line,
+    count_ref,
     mixed,
     staging,
     spread,
     place_ref,
     keep_ref,
     take_ref,
+    small_sem,
     load_sem,
     send_sem,
     recv_sem,
     col_send_sem,
     col_recv_sem,
 ):
-    rows, window_cols = window_ref.shape
+    rows, window_cols = window_hbm.shape
     cols = rest_ref.shape[1]
-    pair_count = pairs_ref.shape[0]
+    pair_count = pairs_hbm.shape[1]
     chunk = STRIP * STRIPS
     chunks = cols // chunk
     tail = cols - chunks * chunk
@@ -96,7 +101,12 @@
                 load_sem.at[chunks],
             )
         )
-    for load in loads:
+    small_loads = [
+        pltpu.make_async_copy(pairs_hbm, pairs_ref, small_sem.at[0]),
+        pltpu.make_async_copy(window_hbm, window_ref, small_sem.at[1]),
+        pltpu.make_async_copy(count_hbm, count_line, small_sem.at[2]),
+    ]
+    for load in small_loads + loads:
         load.start()
 
     barrier = pltpu.get_barrier_semaphore()
@@ -109,13 +119,17 @@
             barrier, inc=1, device_id=(me, lax.rem(my_col + m, col_blocks)), device_id_type=MESH
         )
 
-    survivor_s = pairs_ref[:, 0:1]
-    partner_s = pairs_ref[:, 1:2]
+    small_loads[0].wait()
+    survivor_l = pairs_ref[0:1, :]
+    partner_l = pairs_ref[1:2, :]
     square = (pair_count, pair_count)
     diagonal = iota(square, 0) == iota(square, 1)
 
     def along_lanes(column):
         return jnp.sum(jnp.where(diagonal, column, jnp.zeros_like(column)), axis=0, keepdims=True)
+
+    def down_sublanes(line):
+        return jnp.sum(jnp.where(diagonal, line, jnp.zeros_like(line)), axis=1, keepdims=True)
 
     def block_of(items):
         block = jnp.zeros_like(items)
@@ -123,8 +137,8 @@
             block = block + (items >= b * rows).astype(jnp.int32)
         return block
 
-    survivor_l = along_lanes(survivor_s)
-    partner_l = along_lanes(partner_s)
+    survivor_s = down_sublanes(survivor_l)
+    partner_s = down_sublanes(partner_l)
     src_s, src_l = block_of(partner_s), block_of(partner_l)
     dst_s, dst_l = block_of(survivor_s), block_of(survivor_l)
     same = (src_s * blocks + dst_s) == (src_l * blocks + dst_l)
@@ -159,6 +173,7 @@
             device_id_type=MESH,
         )
 
+    small_loads[1].wait()
     win_rows = send_win.shape[1]
     choose(window_ref[...], window_cols)
     send_win[...] = staging[:, 0:win_rows, :].astype(jnp.bfloat16)
@@ -207,6 +222,8 @@
         preferred_element_type=jnp.float32,
     ).astype(jnp.bfloat16)
 
+    small_loads[2].wait()
+    count_ref[...] = count_line[...].reshape(count_ref.shape)
     lanes_shape = (pair_count, LANES)
 
     def look_up(step, sums):
@@ -343,6 +360,21 @@
         col_copy(my_col, lax.rem(my_col + m, col_blocks)).wait_send()
 
 
+def write_kernel(parts, window_ref, rest_ref, window_out, rest_out, sem):
+    size = rest_ref.shape[0] // parts
+    writes = [
+        pltpu.make_async_copy(
+            rest_ref.at[pl.ds(p * size, size)], rest_out.at[pl.ds(p * size, size)], sem.at[p]
+        )
+        for p in range(parts)
+    ]
+    writes.append(pltpu.make_async_copy(window_ref, window_out, sem.at[parts]))
+    for write in writes:
+        write.start()
+    for write in writes:
+        write.wait()
+
+
 def shards(sim_window, sim_rest, joined_partner_pairs, cluster_member_count):
     blocks = lax.axis_size("row")
     col_blocks = lax.axis_size("col")
@@ -358,13 +390,13 @@
     stage_rows = max(slots * (STRIP // LANES), win_rows)
     bf16, f32 = jnp.bfloat16, jnp.float32
     vmem = pl.BlockSpec(memory_space=pltpu.VMEM)
-    return pl.pallas_call(
+    merged = pl.pallas_call(
         functools.partial(merge_kernel, blocks, col_blocks, slots),
         out_shape=(
             jax.ShapeDtypeStruct(sim_window.shape, bf16),
             jax.ShapeDtypeStruct(sim_rest.shape, bf16),
         ),
-        in_specs=[vmem, pl.BlockSpec(memory_space=pl.ANY), vmem, vmem],
+        in_specs=[pl.BlockSpec(memory_space=pltpu.HBM)] * 4,
         out_specs=(vmem, vmem),
         scratch_shapes=[
             pltpu.VMEM((chunks, blocks, main_rows, LANES), bf16),
@@ -373,12 +405,17 @@
             pltpu.VMEM((blocks, tail_rows, LANES), bf16),
             pltpu.VMEM((blocks, win_rows, LANES), bf16),
             pltpu.VMEM((blocks, win_rows, LANES), bf16),
+            pltpu.VMEM(sim_window.shape, bf16),
+            pltpu.VMEM(joined_partner_pairs.shape[::-1], jnp.int32),
+            pltpu.VMEM(cluster_member_count.shape, jnp.int32),
+            pltpu.VMEM((1, cluster_member_count.shape[0]), jnp.int32),
             pltpu.VMEM((col_blocks, rows, window_cols), bf16),
             pltpu.VMEM((blocks, stage_rows, LANES), f32),
             pltpu.VMEM((blocks, GROUP, STRIP), f32),
             pltpu.VMEM((rows, blocks * GROUP), bf16),
             pltpu.VMEM((rows, LANES), f32),
             pltpu.VMEM((rows, LANES), f32),
+            pltpu.SemaphoreType.DMA((3,)),
             pltpu.SemaphoreType.DMA((chunks + 1,)),
             pltpu.SemaphoreType.DMA((chunks + 2, blocks)),
             pltpu.SemaphoreType.DMA((chunks + 2, blocks)),
@@ -386,10 +423,24 @@
             pltpu.SemaphoreType.DMA((col_blocks,)),
         ],
         compiler_params=pltpu.CompilerParams(
-            collective_id=0, has_side_effects=True, vmem_limit_bytes=44 * 1024 * 1024
+            collective_id=0, has_side_effects=True, vmem_limit_bytes=36 * 1024 * 1024
         ),
         name="merge",
-    )(sim_window, sim_rest, joined_partner_pairs, cluster_member_count.reshape(1, -1))
+    )(sim_window, sim_rest, joined_partner_pairs.T, cluster_member_count)
+    hbm = pl.BlockSpec(memory_space=pltpu.HBM)
+    parts = rows // 16
+    return pl.pallas_call(
+        functools.partial(write_kernel, parts),
+        out_shape=(
+            jax.ShapeDtypeStruct(sim_window.shape, bf16),
+            jax.ShapeDtypeStruct(sim_rest.shape, bf16),
+        ),
+        in_specs=[vmem, vmem],
+        out_specs=(hbm, hbm),
+        scratch_shapes=[pltpu.SemaphoreType.DMA((parts + 1,))],
+        compiler_params=pltpu.CompilerParams(vmem_limit_bytes=4 * 1024 * 1024),
+        name="write",
+    )(*merged)
 
 
 def solution(mesh):

time: 59.2 us -> 48.3 us (0.82)
  local copies, waits for them, and re-layouts: 12.8 us -> 2.28 us
    unnamed x5 -> x6, local copies, waits for them, and re-layouts: 12.1 us -> 2.28 us
    pallas_call x1, Pallas kernels: 45.5 us -> 40.8 us  [shards(): pl.pallas_call(functools.partial(merge_kernel, blocks, col_blocks, slots)...]
    pallas_call x0 -> x1, Pallas kernels: none -> 4.34 us  [shards(): pl.pallas_call(functools.partial(write_kernel, parts), out_shape=(jax.Sha...]
    reshape x1 -> x0, local copies, waits for them, and re-layouts: 0.7 us -> none  [shards(): cluster_member_count.reshape(1, -1)]
where the time goes in v2:
time: 48.3 us; the launch traced here: 48 us
  Pallas kernels  45.1 us (93%)
  local copies, waits for them, and re-layouts  2.28 us (5%)
  between operations  0.65 us (1%)
    pallas_call x1, Pallas kernels, shards(): pl.pallas_call(functools.partial(merge_kernel, blocks, col_blocks, slots)...  40.8 us
    pallas_call x1, Pallas kernels, shards(): pl.pallas_call(functools.partial(write_kernel, parts), out_shape=(jax.Sha...  4.34 us
    unnamed x6, local copies, waits for them, and re-layouts  2.28 us

profile of v2, /device:TPU:0, one launch (start us, length us, event | category | flops | bytes accessed | tf_op | source)
XLA Modules:
  0.0 48.0 jit_solution(7022109572812823911)
XLA Ops:
  0.6 0.0 copy-start
  0.6 0.9 %copy-done = bf16[192,384]{1,0:T(8,128)(2,1)S(1)} copy-done((bf16[192,384]{1,0:T(8,128)(2,1)S(1)}, bf16[192,384]{1,0:T(8,128)(2,1)}, u32[]{:S(2)}) %copy-start) | copy-done | bytes 147480
  1.5 0.0 copy-start.1
  1.5 0.7 %copy-done.1 = s32[1536]{0:T(1024)S(1)} copy-done((s32[1536]{0:T(1024)S(1)}, s32[1536]{0:T(1024)}, u32[]{:S(2)}) %copy-start.1) | copy-done | bytes 6168
  2.2 0.0 copy-start.2
  2.2 0.7 %copy-done.2 = s32[192,2]{0,1:T(2,128)S(1)} copy-done((s32[192,2]{0,1:T(2,128)S(1)}, s32[192,2]{0,1:T(2,128)}, u32[]{:S(2)}) %copy-start.2) | copy-done | bytes 1560
  2.9 40.8 %merge.1 = (bf16[192,384]{1,0:T(8,128)(2,1)S(1)}, bf16[192,29616]{1,0:T(8,128)(2,1)S(1)}) custom-call(bf16[192,384]{1,0:T(8,128)(2,1)S(1)} %copy-done, bf16[192,29616]{1,0:T(8,128)(2,1)} %rest_ref.1, s32[2,192]{1,0:T(2,128)S(1)} %bitcast.1, s32[1536]{0:T(1024)S(1)} %copy-done.1), custom_call_target="tpu_custom_call" | custom-call | tf_op jit(solution)/shard_map/merge/pallas_call | solution.py:393
  43.7 4.3 %write.1 = (bf16[192,384]{1,0:T(8,128)(2,1)}, bf16[192,29616]{1,0:T(8,128)(2,1)}) custom-call(bf16[192,384]{1,0:T(8,128)(2,1)S(1)} %get-tuple-element.4.window_ref, bf16[192,29616]{1,0:T(8,128)(2,1)S(1)} %get-tuple-element.5.rest_ref), custom_call_target="tpu_custom_call" | custom-call | tf_op jit(solution)/shard_map/write/pallas_call | solution.py:432
Async XLA Ops:
  0.6 0.9 %copy-start = (bf16[192,384]{1,0:T(8,128)(2,1)S(1)}, bf16[192,384]{1,0:T(8,128)(2,1)}, u32[]{:S(2)}) copy-start(bf16[192,384]{1,0:T(8,128)(2,1)} %window_hbm.1) | copy-start | bytes 442372
  1.5 0.7 %copy-start.1 = (s32[1536]{0:T(1024)S(1)}, s32[1536]{0:T(1024)}, u32[]{:S(2)}) copy-start(s32[1536]{0:T(1024)} %count_hbm.1) | copy-start | bytes 18436
  2.2 0.7 %copy-start.2 = (s32[192,2]{0,1:T(2,128)S(1)}, s32[192,2]{0,1:T(2,128)}, u32[]{:S(2)}) copy-start(s32[192,2]{0,1:T(2,128)} %param.6) | copy-start | bytes 4612

commit v3 on v2

--- a/solution.py
+++ b/solution.py
@@ -426,7 +426,12 @@
             collective_id=0, has_side_effects=True, vmem_limit_bytes=36 * 1024 * 1024
         ),
         name="merge",
-    )(sim_window, sim_rest, joined_partner_pairs.T, cluster_member_count)
+    )(
+        pltpu.with_memory_space_constraint(sim_window, pltpu.HBM),
+        sim_rest,
+        pltpu.with_memory_space_constraint(joined_partner_pairs.T, pltpu.HBM),
+        pltpu.with_memory_space_constraint(cluster_member_count, pltpu.HBM),
+    )
     hbm = pl.BlockSpec(memory_space=pltpu.HBM)
     parts = rows // 16
     return pl.pallas_call(

time: 48.3 us -> 46.9 us (0.971)
  local copies, waits for them, and re-layouts: 2.28 us -> 0 us
  Pallas kernels: 45.1 us -> 46.1 us
    unnamed x6 -> x0, local copies, waits for them, and re-layouts: 2.28 us -> none
    pallas_call x1, Pallas kernels: 40.8 us -> 41.7 us  [shards(): pl.pallas_call(functools.partial(merge_kernel, blocks, col_blocks, slots)...]
where the time goes in v3:
time: 46.9 us; the launch traced here: 46.7 us
  Pallas kernels  46.1 us (98%)
  between operations  0.64 us (1%)
    pallas_call x1, Pallas kernels, shards(): pl.pallas_call(functools.partial(merge_kernel, blocks, col_blocks, slots)...  41.7 us
    pallas_call x1, Pallas kernels, shards(): pl.pallas_call(functools.partial(write_kernel, parts), out_shape=(jax.Sha...  4.34 us

profile of v3, /device:TPU:0, one launch (start us, length us, event | category | flops | bytes accessed | tf_op | source)
XLA Modules:
  0.0 46.7 jit_solution(7006580049310446476)
XLA Ops:
  0.6 41.7 %merge.1 = (bf16[192,384]{1,0:T(8,128)(2,1)S(1)}, bf16[192,29616]{1,0:T(8,128)(2,1)S(1)}) custom-call(bf16[192,384]{1,0:T(8,128)(2,1)} %window_hbm.1, bf16[192,29616]{1,0:T(8,128)(2,1)} %rest_ref.1, s32[2,192]{1,0:T(2,128)} %bitcast.1, s32[1536]{0:T(1024)} %count_hbm.1), custom_call_target="tpu_custom_call" | custom-call | tf_op jit(solution)/shard_map/merge/pallas_call | solution.py:393
  42.4 4.3 %write.1 = (bf16[192,384]{1,0:T(8,128)(2,1)}, bf16[192,29616]{1,0:T(8,128)(2,1)}) custom-call(bf16[192,384]{1,0:T(8,128)(2,1)S(1)} %get-tuple-element.4.window_ref, bf16[192,29616]{1,0:T(8,128)(2,1)S(1)} %get-tuple-element.5.rest_ref), custom_call_target="tpu_custom_call" | custom-call | tf_op jit(solution)/shard_map/write/pallas_call | solution.py:437
